TPU v7x, 32 devices: a whole 2x2x4 slice. The times are simulated.
32 devices in a mesh: half: 2 (over core), row: 8 (over z, x), col: 2 (over y).
Axes of the slice: x: 2, y: 2, z: 4, core: 2. Of those that a mesh axis runs over, the one named last changes fastest.
Arguments:
- front_matrix: bfloat16 [16384, 2, 2, 4096], P('row', 'col', 'half'), may hold values from -6 to 6
- child_update: bfloat16 [2, 12288, 12288], P('half', 'row', 'col'), may hold values from -6 to 6
- fill_pattern: int32 [2, 96, 96], replicated, may hold values 0 or 1
- child_map: int32 [2, 96], replicated, may hold values from 0 to 127, as said below
- first_inverse: bfloat16 [256, 256], replicated, as said below
- second_inverse: bfloat16 [256, 256], replicated, as said below
Outputs:
- factored: bfloat16 [16384, 2, 2, 4096], P('row', 'col', 'half')
Inputs may be any that keep to these rules, and one draw needn't show every extreme that they name: `child_map`: child block i of each child maps to front block 4 * (i // 3) + t with t in 0 to 3, rising with i inside each group of three; the first child block maps to front block 0 and the last to front block 127. `first_inverse`: entries lie within 1/128 of zero. `second_inverse`: entries lie within 1/128 of zero.
All inputs are finite; a program needn't handle non-finite values.
Results may differ from a plain program's by a relative error of at most 0.002.
Values may be sent and summed in bfloat16 or wider, within the bound.
A program may use at most 256 MiB of HBM per device.

v0:
```python
import jax
import jax.numpy as jnp
from jax import lax
from jax.sharding import PartitionSpec as P

BLOCK = 128
PANEL = 256


def partner(shard, axis, apart):
    return lax.ppermute(shard, axis, [(i, i ^ 1 << apart) for i in range(lax.axis_size(axis))])


def from_root(shard, axis, root):
    mine = lax.axis_index(axis) == root
    return lax.psum(jnp.where(mine, shard, jnp.zeros_like(shard)), axis)


def body(front_matrix, child_update, fill_pattern, child_map, first_inverse, second_inverse):
    rows_local = front_matrix.shape[0]
    slab_width = front_matrix.shape[3]
    child_piece = child_update[0]
    child_rows = child_piece.shape[0]
    child_cols = child_piece.shape[1]
    half_index = lax.axis_index("half")
    row_position = lax.axis_index("row")
    col_position = lax.axis_index("col")
    slab_index = col_position * 2 + half_index
    fanout = lax.axis_size("row") // (2 * lax.axis_size("col"))
    row_blocks_count = child_rows // BLOCK
    half_width = child_cols // 2
    side_blocks = half_width // BLOCK
    front_row_blocks = rows_local // BLOCK
    slab_blocks = slab_width // BLOCK

    def place_blocks(columns, source, target_slab):
        source_map = lax.dynamic_index_in_dim(child_map, source, 0, keepdims=False)
        source_fill = lax.dynamic_index_in_dim(fill_pattern, source, 0, keepdims=False)
        row_start = row_position * row_blocks_count
        col_start = col_position * 2 * side_blocks + (target_slab - 2 * col_position) * side_blocks
        row_targets = lax.dynamic_slice_in_dim(source_map, row_start, row_blocks_count)
        col_targets = lax.dynamic_slice_in_dim(source_map, col_start, side_blocks)
        row_select = (
            row_targets[:, None] - row_position * front_row_blocks
            == jnp.arange(front_row_blocks, dtype=jnp.int32)[None, :]
        ).astype(jnp.bfloat16)
        col_select = (
            col_targets[:, None] - target_slab * slab_blocks
            == jnp.arange(slab_blocks, dtype=jnp.int32)[None, :]
        ).astype(jnp.bfloat16)
        fill_block = lax.dynamic_slice(
            source_fill, (row_start, col_start), (row_blocks_count, side_blocks)
        ).astype(jnp.bfloat16)
        values = columns.reshape(row_blocks_count, BLOCK, side_blocks, BLOCK)
        values = values * fill_block[:, None, :, None]
        moved = jnp.einsum(
            "kq,iakb->iaqb", col_select, values, preferred_element_type=jnp.float32
        ).astype(jnp.bfloat16)
        placed = jnp.einsum("ip,iaqb->paqb", row_select, moved, preferred_element_type=jnp.float32)
        return placed.reshape(rows_local, slab_width)

    own_cols = lax.dynamic_slice_in_dim(child_piece, half_index * half_width, half_width, 1)
    other_cols = lax.dynamic_slice_in_dim(child_piece, (1 - half_index) * half_width, half_width, 1)
    received = partner(other_cols, "half", 0)
    summed = place_blocks(own_cols, half_index, slab_index) + place_blocks(
        received, 1 - half_index, slab_index
    )
    assembled = front_matrix.reshape(rows_local, slab_width).astype(jnp.float32) + summed
    row_index = (row_position * rows_local + jnp.arange(rows_local, dtype=jnp.int32))[:, None]

    def broadcast_panel(lower):
        panel_rows = from_root(lower, ("half", "col"), 0)
        column_parts = []
        for offset in range(fanout):
            column_parts.append(from_root(panel_rows, "row", slab_index * fanout + offset))
        return (panel_rows, jnp.concatenate(column_parts, axis=0))

    first_raw = jnp.dot(
        assembled[:, :PANEL], first_inverse.astype(jnp.float32).T, precision=lax.Precision.HIGHEST
    ).astype(jnp.bfloat16)
    first_low = jnp.where(row_index >= PANEL, first_raw, jnp.zeros_like(first_raw))
    first_rows, first_cols = broadcast_panel(first_low)
    updated = assembled - jnp.dot(first_rows, first_cols.T, preferred_element_type=jnp.float32)
    second_full = jnp.dot(
        updated[:, PANEL : 2 * PANEL],
        second_inverse.astype(jnp.float32).T,
        precision=lax.Precision.HIGHEST,
    )
    second_raw = jnp.where(row_index >= PANEL, second_full, jnp.zeros_like(second_full)).astype(
        jnp.bfloat16
    )
    second_low = jnp.where(row_index >= 2 * PANEL, second_raw, jnp.zeros_like(second_raw))
    second_rows, second_cols = broadcast_panel(second_low)
    final = updated - jnp.dot(second_rows, second_cols.T, preferred_element_type=jnp.float32)
    panels = jnp.concatenate([first_raw, second_raw], axis=1).astype(jnp.float32)
    panel_cols = jnp.where(slab_index == 0, panels, final[:, : 2 * PANEL])
    result = jnp.concatenate([panel_cols, final[:, 2 * PANEL :]], axis=1)
    return result.astype(jnp.bfloat16).reshape(rows_local, 1, 1, slab_width)


def solution(mesh):
    placed = (P("row", "col", "half", None), P("half", "row", "col"), P(), P(), P(), P())
    return jax.shard_map(
        body, mesh=mesh, in_specs=placed, out_specs=P("row", "col", "half", None), check_vma=False
    )
```

profile of v0, /device:TPU:5, one launch (start us, length us, event | category | flops | bytes accessed | tf_op | source)
XLA Modules:
  0.0 586.4 jit_solution(5450581789475958041)
XLA Ops:
  6.5 14.4 %dynamic-slice_bitcast_fusion = (bf16[1536,3072]{1,0:T(8,128)(2,1)}, bf16[192,8,24,128]{3,1,2,0:T(8,128)(2,1)}) fusion(bf16[1,1536,6144]{2,1,0:T(8,128)(2,1)} %param.7, s32[]{:T(128)S(6)} %select_n.97, s32[]{:T(128)S(6)} %select_n.92), kind=kLoop, calls=%fused_computation.17 | loop fusion | bytes 37748744 | tf_op jit(solution)/shard_map/dynamic_slice | solution.py:63
  21.0 0.7 collective-permute-start
  21.7 9.8 %copy.27 = bf16[192,8,24,128]{3,2,1,0:T(8,128)(2,1)} copy(bf16[192,8,24,128]{3,1,2,0:T(8,128)(2,1)} %get-tuple-element.10) | data formatting | bytes 18874368
  31.4 22.4 %copy.11 = bf16[2048,1,1,4096]{0,3,2,1:T(8,128)(2,1)} copy(bf16[2048,1,1,4096]{3,0,2,1:T(8,128)(2,1)} %param.6) | data formatting | bytes 33554432 | tf_op args[0]
  53.9 0.1 subtract_bitcast_fusion
  54.0 0.1 subtract_bitcast_fusion.1
  54.1 0.8 fusion.38
  54.9 11.7 %fusion.11 = bf16[12,128,128,32]{2,3,1,0:T(8,128)(2,1)} fusion(bf16[12,24]{1,0:T(8,128)(2,1)S(1)} %get-tuple-element.16, s32[24]{0:T(128)S(1)} %get-tuple-element.20, bf16[12,128,24,128]{3,2,1,0:T(8,128)(2,1)} %bitcast.76), kind=kOutput, calls=%fused_computation.16 | convolution fusion | flops 306709248 | bytes 22020768 | tf_op jit(solution)/shard_map/kq,iakb->iaqb/dot_general | solution.py:56
  66.5 19.6 %fusion.1 = f32[16,128,32,128]{3,0,2,1:T(8,128)} fusion(bf16[12,128,128,32]{2,3,1,0:T(8,128)(2,1)} %fusion.11, s32[12]{0:T(128)S(1)} %get-tuple-element.18), kind=kOutput, calls=%fused_computation.5 | convolution fusion | flops 201326784 | bytes 46137392 | tf_op jit(solution)/shard_map/ip,iaqb->paqb/dot_general | solution.py:59
  86.1 9.8 %copy.28 = bf16[192,8,24,128]{3,2,1,0:T(8,128)(2,1)} copy(bf16[192,8,24,128]{3,1,2,0:T(8,128)(2,1)} %bitcast.29) | data formatting | bytes 18874368
  95.9 11.6 %fusion.10 = bf16[12,128,128,32]{2,3,1,0:T(8,128)(2,1)} fusion(bf16[12,24]{1,0:T(8,128)(2,1)S(1)} %get-tuple-element.15, s32[24]{0:T(128)S(1)} %get-tuple-element.19, bf16[12,128,24,128]{3,2,1,0:T(8,128)(2,1)} %bitcast.77), kind=kOutput, calls=%fused_computation.14 | convolution fusion | flops 306709248 | bytes 22020768 | tf_op jit(solution)/shard_map/kq,iakb->iaqb/dot_general | solution.py:56
  107.5 29.2 %fusion.7 = f32[16,128,32,128]{3,0,2,1:T(8,128)} fusion(f32[16,128,32,128]{3,0,2,1:T(8,128)} %fusion.1, bf16[12,128,128,32]{2,3,1,0:T(8,128)(2,1)} %fusion.10, s32[12]{0:T(128)S(1)} %get-tuple-element.17), kind=kOutput, calls=%fused_computation.12 | convolution fusion | flops 209715392 | bytes 79691824 | tf_op jit(solution)/shard_map/ip,iaqb->paqb/dot_general | solution.py:59
  136.7 33.8 %copy.25 = f32[16,128,32,128]{1,0,3,2:T(8,128)} copy(f32[16,128,32,128]{3,0,2,1:T(8,128)} %fusion.7) | data formatting | bytes 67108864 | tf_op jit(solution)/shard_map/add | solution.py:65
  170.5 23.0 %bitcast_add_fusion = f32[2048,4096]{0,1:T(8,128)S(1)} fusion(f32[512,8,16,128]{3,2,1,0:T(8,128)} %bitcast.75, bf16[2048,1,1,4096]{0,3,2,1:T(8,128)(2,1)} %copy.11), kind=kLoop, calls=%fused_computation | loop fusion | flops 16777216 | bytes 83886080 | tf_op jit(solution)/shard_map/add | solution.py:68
  193.6 11.1 %copy-done.1 = f32[2048,4096]{0,1:T(8,128)} copy-done((f32[2048,4096]{0,1:T(8,128)}, f32[2048,4096]{0,1:T(8,128)S(1)}, u32[]{:S(2)}) %copy-start.1) | copy-done | bytes 33554456
  204.7 2.3 select_select_fusion.1
  206.9 0.0 all-reduce.13.cloned.1.call-start
  207.0 36.2 %all-reduce.7.cloned.1.call-done = bf16[2048,256]{0,1:T(8,128)(2,1)} async-done(((bf16[2048,256]{0,1:T(8,128)(2,1)}), bf16[2048,256]{0,1:T(8,128)(2,1)}) %all-reduce.7.cloned.1.call-update) | async-done | bytes 1048592 | tf_op jit(solution)/shard_map/psum | solution.py:16
  243.2 2.7 broadcast_select_fusion.3
  245.9 0.0 all-reduce.9.cloned.1.call-start
  246.0 104.4 %all-reduce.13.cloned.1.call-done = (bf16[2048,256]{0,1:T(8,128)(2,1)}, bf16[2048,256]{0,1:T(8,128)(2,1)}) async-done(((bf16[2048,256]{0,1:T(8,128)(2,1)}, bf16[2048,256]{0,1:T(8,128)(2,1)}), (bf16[2048,256]{0,1:T(8,128)(2,1)}, bf16[2048,256]{0,1:T(8,128)(2,1)})) %all-reduce.13.cloned.1.call-update) | async-done | bytes 2097168 | tf_op jit(solution)/shard_map/psum | solution.py:16
  350.3 25.5 %convolution_subtract_fusion.1 = f32[2048,4096]{0,1:T(8,128)} fusion(f32[2048,4096]{0,1:T(8,128)} %copy-done.1, bf16[2048,256]{0,1:T(8,128)(2,1)} %all-reduce.7.cloned.1.call-done, bf16[2048,256]{0,1:T(8,128)(2,1)} %get-tuple-element.7, bf16[2048,256]{0,1:T(8,128)(2,1)} %get-tuple-element.8), kind=kOutput, calls=%fused_computation.10 | convolution fusion | flops 4307550208 | bytes 70254592 | tf_op jit(solution)/shard_map/dot_general | solution.py:83
  375.9 3.9 select_select_fusion
  379.8 0.0 all-reduce.11.cloned.1.call-start
  379.8 35.5 %all-reduce.9.cloned.1.call-done = bf16[2048,256]{0,1:T(8,128)(2,1)} async-done(((bf16[2048,256]{0,1:T(8,128)(2,1)}), bf16[2048,256]{0,1:T(8,128)(2,1)}) %all-reduce.9.cloned.1.call-update) | async-done | bytes 1048592 | tf_op jit(solution)/shard_map/psum | solution.py:16
  415.3 2.7 broadcast_select_fusion.2
  418.1 103.8 %all-reduce.11.cloned.1.call-done = (bf16[2048,256]{0,1:T(8,128)(2,1)}, bf16[2048,256]{0,1:T(8,128)(2,1)}) async-done(((bf16[2048,256]{0,1:T(8,128)(2,1)}, bf16[2048,256]{0,1:T(8,128)(2,1)}), (bf16[2048,256]{0,1:T(8,128)(2,1)}, bf16[2048,256]{0,1:T(8,128)(2,1)})) %all-reduce.11.cloned.1.call-update) | async-done | bytes 2097168 | tf_op jit(solution)/shard_map/psum | solution.py:16
  521.9 19.1 %convolution_subtract_fusion = bf16[2048,4096]{0,1:T(8,128)(2,1)} fusion(f32[2048,4096]{0,1:T(8,128)} %convolution_subtract_fusion.1, bf16[2048,256]{0,1:T(8,128)(2,1)} %all-reduce.9.cloned.1.call-done, bf16[2048,256]{0,1:T(8,128)(2,1)} %get-tuple-element.5, bf16[2048,256]{0,1:T(8,128)(2,1)} %get-tuple-element.6), kind=kOutput, calls=%fused_computation.9 | convolution fusion | flops 4315938816 | bytes 53477376 | tf_op jit(solution)/shard_map/dot_general | solution.py:94
  541.0 7.7 %fusion.6 = bf16[2048,1,1,3584]{0,3,2,1:T(8,128)(2,1)S(1)} fusion(bf16[2048,4096]{0,1:T(8,128)(2,1)} %convolution_subtract_fusion), kind=kLoop, calls=%fused_computation.11 | loop fusion | bytes 29360128 | tf_op jit(solution)/shard_map/concatenate | solution.py:97
  548.8 2.4 fusion.16
  551.2 7.5 %pad_maximum_fusion = bf16[2048,1,1,4096]{0,3,2,1:T(8,128)(2,1)} fusion(bf16[2048,1,1,3584]{0,3,2,1:T(8,128)(2,1)S(1)} %fusion.6, bf16[2048,1,1,512]{0,3,2,1:T(8,128)(2,1)S(1)} %fusion.16), kind=kLoop, calls=%fused_computation.8 | loop fusion | flops 33554432 | bytes 33554432 | tf_op jit(solution)/shard_map/concatenate | solution.py:97
  558.7 21.2 %copy.16 = bf16[2048,1,1,4096]{3,0,2,1:T(8,128)(2,1)} copy(bf16[2048,1,1,4096]{0,3,2,1:T(8,128)(2,1)} %pad_maximum_fusion) | data formatting | bytes 33554432 | tf_op jit(solution)/shard_map/concatenate | solution.py:97
  (15 shorter events, 0.1 us)
Async XLA Ops:
  6.5 198.1 %copy-start = (bf16[256,256]{1,0:T(8,128)(2,1)S(1)}, bf16[256,256]{1,0:T(8,128)(2,1)}, u32[]{:S(2)}) copy-start(bf16[256,256]{1,0:T(8,128)(2,1)} %param.10) | copy-start | bytes 393220
  6.5 236.6 %all-reduce.7.cloned.1.call-start = ((), (), s32[]{:S(2)}) async-start(), calls=%async_computation | async-start | bytes 2097152 | tf_op jit(solution)/shard_map/psum | solution.py:16
  21.0 65.1 %collective-permute-start = (bf16[1536,3072]{1,0:T(8,128)(2,1)}, bf16[1536,3072]{1,0:T(8,128)(2,1)}, u32[]{:S(2)}, u32[]{:S(2)}) collective-permute-start(bf16[1536,3072]{1,0:T(8,128)(2,1)} %get-tuple-element.9), channel_id=1, source_target_pairs={{0,16},{16,0},{1,17},{17,1},{2,18},{18,2},{3,19},{19,3},{4,20},{20... | collective-permute-start | bytes 28311560 | tf_op jit(solution)/shard_map/ppermute | solution.py:11
  31.4 22.4 %copy-start.2 = (s32[2,96]{1,0:T(2,128)S(1)}, s32[2,96]{1,0:T(2,128)}, u32[]{:S(2)}) copy-start(s32[2,96]{1,0:T(2,128)} %param.9) | copy-start | bytes 2308
  193.6 11.1 %copy-start.1 = (f32[2048,4096]{0,1:T(8,128)}, f32[2048,4096]{0,1:T(8,128)S(1)}, u32[]{:S(2)}) copy-start(f32[2048,4096]{0,1:T(8,128)S(1)} %bitcast_add_fusion) | copy-start | bytes 100663296
  206.9 143.4 %all-reduce.13.cloned.1.call-start = ((), (), s32[]{:S(2)}) async-start(), calls=%async_computation.3 | async-start | bytes 4194304 | tf_op jit(solution)/shard_map/psum | solution.py:16
  245.9 169.4 %all-reduce.9.cloned.1.call-start = ((), (), s32[]{:S(2)}) async-start(), calls=%async_computation.1 | async-start | bytes 2097152 | tf_op jit(solution)/shard_map/psum | solution.py:16
  350.3 25.5 %copy-start.3 = (bf16[256,256]{1,0:T(8,128)(2,1)S(1)}, bf16[256,256]{1,0:T(8,128)(2,1)}, u32[]{:S(2)}) copy-start(bf16[256,256]{1,0:T(8,128)(2,1)} %param.11) | copy-start | bytes 393220
  379.8 142.2 %all-reduce.11.cloned.1.call-start = ((), (), s32[]{:S(2)}) async-start(), calls=%async_computation.2 | async-start | bytes 4194304 | tf_op jit(solution)/shard_map/psum | solution.py:16
Sparse Core Ops, SparseCore 0:
  207.1 36.0 all-reduce.6
  247.3 103.0 all-reduce.12
  379.9 35.3 all-reduce.8
  418.9 103.0 all-reduce.10
where the time goes:
time: 590 us; the launch traced here: 586 us
  waiting for transfers between devices  280 us (47%)
  local copies, waits for them, and re-layouts  130 us (22%)
  matrix products  123 us (21%)
  other arithmetic  39.4 us (7%)
  between operations  13.2 us (2%)
    psum x4, waiting for transfers between devices, from_root(): return lax.psum(jnp.where(mine, shard, jnp.zeros_like(shard)), axis)  280 us
    unnamed x11, local copies, waits for them, and re-layouts  53.1 us
    dot_general x2, matrix products, place_blocks(): jnp.einsum('ip,iaqb->paqb', row_select, moved, preferred_element_type=jnp...  48.8 us
    add x1, local copies, waits for them, and re-layouts, body(): place_blocks(own_cols, half_index, slab_index)  33.8 us
    concatenate x2, local copies, waits for them, and re-layouts, body(): result = jnp.concatenate([panel_cols, final[:, 2 * PANEL:]], axis=1)  28.9 us
    dot_general x1, matrix products, body(): jnp.dot(first_rows, first_cols.T, preferred_element_type=jnp.float32)  25.5 us
    dot_general x2, matrix products, place_blocks(): jnp.einsum('kq,iakb->iaqb', col_select, values, preferred_element_type=jn...  23.3 us
    add x1, other arithmetic, body(): front_matrix.reshape(rows_local, slab_width).astype(jnp.float32) + summed  23 us
  transfers between devices with their start and end apart: 5, of which 4 were waited for; matrix products, arithmetic and copies ran while one was open for 11% of the time, Pallas kernels for 0%

commit v1 on v0

v1 whole, which is shorter than its diff:
```python
import functools

import jax
import jax.numpy as jnp
from jax import lax
from jax.experimental import pallas as pl
from jax.experimental.pallas import tpu as pltpu
from jax.sharding import PartitionSpec as P

BLOCK = 128
PANEL = 256
BOTH = 2 * PANEL
GROUP = 3 * BLOCK
CHUNKS = 4
MESH_IDS = pl.DeviceIdType.MESH
F32 = jnp.float32
BF16 = jnp.bfloat16


def dot_t(a, b):
    return lax.dot_general(a, b, (((1,), (1,)), ((), ())), preferred_element_type=F32)


def dot_exact(a, b):
    high = a.astype(BF16)
    rest = a - high.astype(F32)
    mid = rest.astype(BF16)
    low = (rest - mid.astype(F32)).astype(BF16)
    return dot_t(low, b) + dot_t(mid, b) + dot_t(high, b)


def locate(cmap, source, group, slot):
    target = 4 * group + slot
    m0 = cmap[source, 3 * group]
    m1 = cmap[source, 3 * group + 1]
    m2 = cmap[source, 3 * group + 2]
    k = jnp.where(m1 <= target, 1, 0)
    k = jnp.where(m2 <= target, 2, k)
    hit = (m0 == target) | (m1 == target) | (m2 == target)
    return k, hit


def panel_kernel(
    n_half, n_row, n_col,
    front, child, fill, cmap, inverse1, inverse2,
    received, lrows, lcols, raw,
    front_v, own_v, other_v, asm, l_v, raw_v, top_v,
    load_sem, early_send, early_recv, late_send, late_recv, top_send, top_recv,
    row_send, row_recv, line_send, line_recv, lane_send, lane_recv, out_sem,
):
    rows = front.shape[0]
    half_width = received.shape[1]
    chunk = rows // CHUNKS
    fanout = n_row // (2 * n_col)
    n_z = n_row // fanout
    h, r, c = lax.axis_index("half"), lax.axis_index("row"), lax.axis_index("col")
    slab = 2 * c + h
    z, lane = lax.div(r, fanout), lax.rem(r, fanout)
    root = slab == 0

    barrier = pltpu.get_barrier_semaphore()
    pl.semaphore_signal(barrier, inc=1, device_id={"half": 1 - h}, device_id_type=MESH_IDS)
    for k in range(1, n_col):
        pl.semaphore_signal(
            barrier, inc=1, device_id={"col": lax.rem(c + k, n_col)}, device_id_type=MESH_IDS
        )
    for k in range(1, n_row):
        pl.semaphore_signal(
            barrier, inc=1, device_id={"row": lax.rem(r + k, n_row)}, device_id_type=MESH_IDS
        )
    load_front = pltpu.make_async_copy(front.at[:, pl.ds(0, BOTH)], front_v, load_sem.at[0])
    load_own = pltpu.make_async_copy(child.at[:, pl.ds(0, GROUP)], own_v, load_sem.at[1])

    @pl.when(root)
    def _():
        load_front.start()
        load_own.start()

    pl.semaphore_wait(barrier, 1 + (n_col - 1) + (n_row - 1))

    early = pltpu.make_async_remote_copy(
        src_ref=child.at[:, pl.ds(0, GROUP)], dst_ref=other_v,
        send_sem=early_send, recv_sem=early_recv,
        device_id={"half": 1 - h}, device_id_type=MESH_IDS,
    )
    start = pl.multiple_of((1 - h) * half_width, 128)
    late = pltpu.make_async_remote_copy(
        src_ref=child.at[:, pl.ds(start, half_width)], dst_ref=received,
        send_sem=late_send, recv_sem=late_recv,
        device_id={"half": 1 - h}, device_id_type=MESH_IDS,
    )

    @pl.when(slab == 1)
    def _():
        early.start()

    late.start()

    def part(ref, k):
        return ref.at[pl.ds(k * chunk, chunk), :]

    def slot_part(ref, k):
        return ref.at[pl.ds(pl.multiple_of(lane * rows + k * chunk, chunk), chunk), :]

    def to_col(k, j):
        return pltpu.make_async_remote_copy(
            src_ref=part(l_v, k), dst_ref=part(lrows, k),
            send_sem=row_send.at[j, k], recv_sem=row_recv.at[k],
            device_id={"col": j}, device_id_type=MESH_IDS,
        )

    def to_half(k, src):
        return pltpu.make_async_remote_copy(
            src_ref=part(src, k), dst_ref=part(lrows, k),
            send_sem=row_send.at[0, k], recv_sem=row_recv.at[k],
            device_id={"half": 1 - h}, device_id_type=MESH_IDS,
        )

    def to_line(k, step, src):
        return pltpu.make_async_remote_copy(
            src_ref=src, dst_ref=slot_part(lcols, k),
            send_sem=line_send.at[(step + 1) // 2, k], recv_sem=line_recv.at[k],
            device_id={"row": r + step * fanout}, device_id_type=MESH_IDS,
        )

    def to_lane(k, d, src):
        return pltpu.make_async_remote_copy(
            src_ref=src, dst_ref=slot_part(lcols, k),
            send_sem=lane_send.at[d, k], recv_sem=lane_recv.at[d, k],
            device_id={"row": z * fanout + lax.rem(lane + d, fanout)}, device_id_type=MESH_IDS,
        )

    def keep_rows(k):
        return pltpu.make_async_copy(part(l_v, k), part(lrows, k), out_sem.at[0, k])

    def keep_raw(k):
        return pltpu.make_async_copy(part(raw_v, k), part(raw, k), out_sem.at[1, k])

    def keep_cols(k, src):
        return pltpu.make_async_copy(part(src, k), slot_part(lcols, k), out_sem.at[2, k])

    def send_cols(k, src, src_slot):
        @pl.when(z + 1 < n_z)
        def _():
            to_line(k, 1, part(src, k)).start()

        @pl.when(z >= 1)
        def _():
            to_line(k, -1, part(src, k)).start()

        for d in range(1, fanout):
            to_lane(k, d, part(src, k)).start()
        keep_cols(k, src).start()

    @pl.when(root)
    def _():
        load_front.wait()
        load_own.wait()
        early.wait_recv()
        groups = rows // BOTH

        def lands(source, index, target):
            apart = cmap[source, index] - target
            return 1 - jnp.minimum(apart * apart, 1)

        def assemble(g, carry):
            group = r * groups + g
            for t in range(4):
                row0 = pl.multiple_of(g * BOTH + t * BLOCK, BLOCK)
                for q in range(4):
                    total = front_v[pl.ds(row0, BLOCK), q * BLOCK : (q + 1) * BLOCK].astype(F32)
                    for source, piece in ((0, own_v), (1, other_v)):
                        for kr in range(max(t - 1, 0), min(t, 2) + 1):
                            hit_r = lands(source, 3 * group + kr, 4 * group + t)
                            for kc in range(max(q - 1, 0), min(q, 2) + 1):
                                hit = hit_r * lands(source, kc, q) * fill[source, 3 * group + kr, kc]
                                block = piece[
                                    pl.ds(pl.multiple_of(g * GROUP + kr * BLOCK, BLOCK), BLOCK),
                                    kc * BLOCK : (kc + 1) * BLOCK,
                                ]
                                total = total + block.astype(F32) * hit.astype(F32)
                    asm[pl.ds(row0, BLOCK), q * BLOCK : (q + 1) * BLOCK] = total
            return carry

        lax.fori_loop(0, groups, assemble, 0)

        step_rows = PANEL

        def first(k, carry):
            row0 = pl.multiple_of(k * step_rows, step_rows)
            value = dot_exact(asm[pl.ds(row0, step_rows), 0:PANEL], inverse1[...]).astype(BF16)
            raw_v[pl.ds(row0, step_rows), 0:PANEL] = value
            keep = r * rows + row0 >= PANEL
            l_v[pl.ds(row0, step_rows), 0:PANEL] = jnp.where(keep, value, jnp.zeros_like(value))
            return carry

        lax.fori_loop(0, rows // step_rows, first, 0)

        def to_top(j):
            return pltpu.make_async_remote_copy(
                src_ref=top_v, dst_ref=top_v, send_sem=top_send.at[j], recv_sem=top_recv,
                device_id={"row": j}, device_id_type=MESH_IDS,
            )

        @pl.when(r == 0)
        def _():
            top_v[...] = raw_v[PANEL:BOTH, 0:PANEL]
            for j in range(1, n_row):
                to_top(j).start()

        @pl.when(r != 0)
        def _():
            to_top(0).wait_recv()

        for k in range(CHUNKS):

            def second(i, carry):
                row0 = pl.multiple_of(k * chunk + i * step_rows, step_rows)
                here = pl.ds(row0, step_rows)
                updated = asm[here, PANEL:BOTH] - dot_t(l_v[here, 0:PANEL], top_v[...])
                value = dot_exact(updated, inverse2[...]).astype(BF16)
                none = jnp.zeros_like(value)
                raw_v[here, PANEL:BOTH] = jnp.where(r * rows + row0 >= PANEL, value, none)
                l_v[here, PANEL:BOTH] = jnp.where(r * rows + row0 >= BOTH, value, none)
                return carry

            lax.fori_loop(0, chunk // step_rows, second, 0)
            for j in range(1, n_col):
                to_col(k, j).start()
            to_half(k, l_v).start()
            keep_rows(k).start()
            keep_raw(k).start()

            @pl.when(z == slab)
            def _():
                send_cols(k, l_v, None)

        @pl.when(r == 0)
        def _():
            for j in range(1, n_row):
                to_top(j).wait_send()

    for k in range(CHUNKS):

        @pl.when(slab != 0)
        def _():
            to_half(k, lrows).wait_recv()

            @pl.when((h == 0) & (c != 0))
            def _():
                to_half(k, lrows).start()

            @pl.when(z == slab)
            def _():
                send_cols(k, lrows, None)

        @pl.when(z != slab)
        def _():
            here = slot_part(lcols, k)
            to_line(k, 1, here).wait_recv()

            @pl.when((z > slab) & (z + 1 < n_z))
            def _():
                to_line(k, 1, here).start()

            @pl.when((z < slab) & (z >= 1))
            def _():
                to_line(k, -1, here).start()

            for d in range(1, fanout):
                to_lane(k, d, here).start()

    for k in range(CHUNKS):
        here = slot_part(lcols, k)
        for d in range(1, fanout):
            other = lax.rem(lane + fanout - d, fanout)
            landed = lcols.at[pl.ds(pl.multiple_of(other * rows + k * chunk, chunk), chunk), :]
            pltpu.make_async_remote_copy(
                src_ref=landed, dst_ref=landed, send_sem=lane_send.at[d, k],
                recv_sem=lane_recv.at[d, k], device_id={"half": 1 - h}, device_id_type=MESH_IDS,
            ).wait_recv()
            to_lane(k, d, here).wait_send()

        @pl.when(root)
        def _():
            for j in range(1, n_col):
                to_col(k, j).wait_send()
            keep_rows(k).wait()
            keep_raw(k).wait()

        @pl.when(h == 0)
        def _():
            to_half(k, lrows).wait_send()

        @pl.when((z >= slab) & (z + 1 < n_z))
        def _():
            to_line(k, 1, here).wait_send()

        @pl.when((z <= slab) & (z >= 1))
        def _():
            to_line(k, -1, here).wait_send()

        @pl.when(z == slab)
        def _():
            keep_cols(k, lrows).wait()

    @pl.when(slab == 1)
    def _():
        early.wait_send()

    late.wait()


def update_kernel(
    place, cmap, fill, front, own, other, lrows, lcols, raw, out, product
):
    half, slab, row_group0, col_group0 = place[0], place[1], place[2], place[3]
    j, i = pl.program_id(0), pl.program_id(1)
    tile_cols = front.shape[1]
    product[...] = dot_t(lrows[...], lcols[...])
    row_group = row_group0 + i
    pieces = ((half, own), (1 - half, other))
    row_spots = [[locate(cmap, source, row_group, p) for p in range(4)] for source, _ in pieces]
    for q in range(tile_cols // BLOCK):
        col_group = col_group0 + j * (tile_cols // BOTH) + q // 4
        col_spots = [locate(cmap, source, col_group, q % 4) for source, _ in pieces]
        columns = slice(q * BLOCK, (q + 1) * BLOCK)
        for p in range(4):
            here = slice(p * BLOCK, (p + 1) * BLOCK)
            total = front[here, columns].astype(F32)
            for n, (source, piece) in enumerate(pieces):
                kr, hit_r = row_spots[n][p]
                kc, hit_c = col_spots[n]
                use = hit_r & hit_c & (fill[source, 3 * row_group + kr, 3 * col_group + kc] != 0)
                block = piece[
                    pl.ds(pl.multiple_of(kr * BLOCK, BLOCK), BLOCK),
                    pl.ds(pl.multiple_of(q // 4 * GROUP + kc * BLOCK, BLOCK), BLOCK),
                ]
                total = total + jnp.where(use, block.astype(F32), 0.0)
            out[here, columns] = (total - product[here, columns]).astype(BF16)

    @pl.when((slab == 0) & (j == 0))
    def _():
        out[:, 0:BOTH] = raw[...]


def body(sizes, front_matrix, child_update, fill_pattern, child_map, first_inverse, second_inverse):
    n_half, n_row, n_col = sizes
    rows, width = front_matrix.shape[0], front_matrix.shape[3]
    front = front_matrix.reshape(rows, width)
    child = child_update.reshape(child_update.shape[1:])
    child_rows, half_width = child.shape[0], child.shape[1] // 2
    fanout = n_row // (2 * n_col)
    any_space = pl.BlockSpec(memory_space=pl.ANY)
    smem = pl.BlockSpec(memory_space=pltpu.SMEM)
    vmem = pl.BlockSpec(memory_space=pltpu.VMEM)
    dma = pltpu.SemaphoreType.DMA
    received, lrows, lcols, raw = pl.pallas_call(
        functools.partial(panel_kernel, n_half, n_row, n_col),
        out_shape=[
            jax.ShapeDtypeStruct((child_rows, half_width), BF16),
            jax.ShapeDtypeStruct((rows, BOTH), BF16),
            jax.ShapeDtypeStruct((width, BOTH), BF16),
            jax.ShapeDtypeStruct((rows, BOTH), BF16),
        ],
        in_specs=[any_space, any_space, smem, smem, vmem, vmem],
        out_specs=[any_space] * 4,
        scratch_shapes=[
            pltpu.VMEM((rows, BOTH), BF16),
            pltpu.VMEM((child_rows, GROUP), BF16),
            pltpu.VMEM((child_rows, GROUP), BF16),
            pltpu.VMEM((rows, BOTH), F32),
            pltpu.VMEM((rows, BOTH), BF16),
            pltpu.VMEM((rows, BOTH), BF16),
            pltpu.VMEM((PANEL, PANEL), BF16),
            dma((2,)), dma, dma, dma, dma, dma((n_row,)), dma,
            dma((n_col, CHUNKS)), dma((CHUNKS,)),
            dma((2, CHUNKS)), dma((CHUNKS,)),
            dma((fanout, CHUNKS)), dma((fanout, CHUNKS)), dma((3, CHUNKS)),
        ],
        compiler_params=pltpu.CompilerParams(
            collective_id=0, has_side_effects=True, vmem_limit_bytes=40 * 2**20
        ),
        name="panels",
    )(front, child, fill_pattern, child_map, first_inverse, second_inverse)

    half = lax.axis_index("half")
    row = lax.axis_index("row")
    slab = lax.axis_index("col") * 2 + half
    place = jnp.stack([half, slab, row * (rows // BOTH), slab * (width // BOTH)]).astype(jnp.int32)
    tile = 2 * BOTH
    tile_child = 2 * GROUP
    halves = half_width // tile_child
    out = pl.pallas_call(
        update_kernel,
        out_shape=jax.ShapeDtypeStruct((rows, width), BF16),
        grid_spec=pltpu.PrefetchScalarGridSpec(
            num_scalar_prefetch=3,
            grid=(width // tile, rows // BOTH),
            in_specs=[
                pl.BlockSpec((BOTH, tile), lambda j, i, *_: (i, j)),
                pl.BlockSpec((GROUP, tile_child), lambda j, i, place, *_: (i, place[0] * halves + j)),
                pl.BlockSpec((GROUP, tile_child), lambda j, i, *_: (i, j)),
                pl.BlockSpec((BOTH, BOTH), lambda j, i, *_: (i, 0)),
                pl.BlockSpec((tile, BOTH), lambda j, i, *_: (j, 0)),
                pl.BlockSpec((BOTH, BOTH), lambda j, i, *_: (i, 0)),
            ],
            out_specs=pl.BlockSpec((BOTH, tile), lambda j, i, *_: (i, j)),
            scratch_shapes=[pltpu.VMEM((BOTH, tile), F32)],
        ),
        compiler_params=pltpu.CompilerParams(vmem_limit_bytes=48 * 2**20),
        name="update",
    )(place, child_map, fill_pattern, front, child, received, lrows, lcols, raw)
    return out.reshape(rows, 1, 1, width)


def solution(mesh):
    placed = (P("row", "col", "half", None), P("half", "row", "col"), P(), P(), P(), P())
    sizes = (mesh.shape["half"], mesh.shape["row"], mesh.shape["col"])
    return jax.shard_map(
        functools.partial(body, sizes), mesh=mesh, in_specs=placed,
        out_specs=P("row", "col", "half", None), check_vma=False,
    )
```

time: 590 us -> 143 us (0.24)
  waiting for transfers between devices: 280 us -> 0 us
  Pallas kernels: 0 us -> 137 us
  local copies, waits for them, and re-layouts: 130 us -> 5.45 us
  matrix products: 123 us -> 0 us
  other arithmetic: 39.4 us -> 0.08 us
  between operations: 13.2 us -> 0.02 us
    psum x4 -> x0, waiting for transfers between devices: 280 us -> none  [from_root(): return lax.psum(jnp.where(mine, shard, jnp.zeros_like(shard)), axis)]
    pallas_call x0 -> x2, Pallas kernels: none -> 137 us  [the longest x1 106 us: body(): pl.pallas_call(functools.partial(panel_kernel, n_half, n_row, n_col), out...]
    dot_general x8 -> x0, matrix products: 123 us -> none  [the longest x2 48.8 us: place_blocks(): jnp.einsum('ip,iaqb->paqb', row_select, moved, preferred_element_type=jnp...]
    unnamed x11 -> x14, local copies, waits for them, and re-layouts: 53.1 us -> 5.45 us
    add x1 -> x0, local copies, waits for them, and re-layouts: 33.8 us -> none  [body(): place_blocks(own_cols, half_index, slab_index)]
    concatenate x2 -> x0, local copies, waits for them, and re-layouts: 28.9 us -> none  [body(): result = jnp.concatenate([panel_cols, final[:, 2 * PANEL:]], axis=1)]
    add x1 -> x0, other arithmetic: 23 us -> none  [body(): front_matrix.reshape(rows_local, slab_width).astype(jnp.float32) + summed]
    dynamic_slice x1 -> x0, local copies, waits for them, and re-layouts: 14.4 us -> none  [body(): lax.dynamic_slice_in_dim(child_piece, (1 - half_index) * half_width, half...]
  transfers between devices with their start and end apart: 5 -> 0, of which waited for: 4 -> 0; matrix products, arithmetic and copies ran while one was open for 11% -> 0% of each run, Pallas kernels for 0% -> 0%
where the time goes in v1:
time: 143 us; the launch traced here: 142 us
  Pallas kernels  137 us (96%)
  local copies, waits for them, and re-layouts  5.45 us (4%)
    pallas_call x1, Pallas kernels, body(): pl.pallas_call(functools.partial(panel_kernel, n_half, n_row, n_col), out...  106 us
    pallas_call x1, Pallas kernels, body(): pl.pallas_call(update_kernel, out_shape=jax.ShapeDtypeStruct((rows, width...  30.4 us
    unnamed x14, local copies, waits for them, and re-layouts  5.45 us

profile of v1, /device:TPU:5, one launch (start us, length us, event | category | flops | bytes accessed | tf_op | source)
XLA Modules:
  0.0 142.3 jit_solution(15056229710235956968)
XLA Ops:
  0.0 0.1 pad_add_fusion.place
  0.1 0.0 copy-start.1
  0.1 0.9 copy-done.1
  1.0 0.0 copy-start.3
  1.0 0.9 copy-done.3
  1.9 0.0 copy-start.4
  1.9 0.9 copy-done.4
  2.8 0.0 copy-start.5
  2.8 0.7 copy-done.5
  3.5 0.0 copy-start.2
  3.5 0.0 copy-start.6
  3.5 106.4 %panels.1 = (bf16[1536,3072]{1,0:T(8,128)(2,1)}, bf16[2048,512]{1,0:T(8,128)(2,1)S(1)}, bf16[4096,512]{1,0:T(8,128)(2,1)S(1)}, bf16[2048,512]{1,0:T(8,128)(2,1)S(1)}) custom-call(bf16[2048,4096]{1,0:T(8,128)(2,1)} %bitcast.9, bf16[1536,6144]{1,0:T(8,128)(2,1)} %bitcast.7, s32[2,96,96]{2,1,0:T(8,128)S(1)} %copy-done.1, s32[2,96]{1,0:T(2,128)S(1)} %copy-done.5, ...), custom_call_target="tpu_custom_call" | custom-call | tf_op jit(solution)/shard_map/panels/pallas_call | solution.py:358
  109.8 0.0 copy-start
  109.9 2.1 %copy-done = bf16[4096,512]{1,0:T(8,128)(2,1)} copy-done((bf16[4096,512]{1,0:T(8,128)(2,1)}, bf16[4096,512]{1,0:T(8,128)(2,1)S(1)}, u32[]{:S(2)}) %copy-start) | copy-done | bytes 4194328
  111.9 0.0 copy-done.2
  111.9 0.0 copy-done.6
  111.9 30.4 %update.1 = bf16[2048,4096]{1,0:T(8,128)(2,1)} custom-call(s32[4]{0:T(128)S(1)} %pad_add_fusion.place, s32[2,96]{1,0:T(2,128)S(1)} %copy-done.6, s32[2,96,96]{2,1,0:T(8,128)S(1)} %copy-done.2, bf16[2048,4096]{1,0:T(8,128)(2,1)} %bitcast.10, bf16[1536,6144]{1,0:T(8,128)(2,1)} %bitcast.8, bf16[1536,3072]{1,0:T(8,128)(2,1)} %get-tuple-element.9.other, ...), custom_call_target="tpu_custom_call" | custom-call | tf_op jit(solution)/shard_map/update/pallas_call | solution.py:394
Async XLA Ops:
  0.1 0.9 copy-start.1
  1.0 0.9 copy-start.3
  1.9 0.9 copy-start.4
  2.8 0.7 copy-start.5
  3.5 108.5 %copy-start.2 = (s32[2,96,96]{2,1,0:T(8,128)S(1)}, s32[2,96,96]{2,1,0:T(8,128)}, u32[]{:S(2)}) copy-start(s32[2,96,96]{2,1,0:T(8,128)} %fill.3) | copy-start | bytes 221188
  3.5 108.5 %copy-start.6 = (s32[2,96]{1,0:T(2,128)S(1)}, s32[2,96]{1,0:T(2,128)}, u32[]{:S(2)}) copy-start(s32[2,96]{1,0:T(2,128)} %cmap.3) | copy-start | bytes 2308
  109.8 2.1 %copy-start = (bf16[4096,512]{1,0:T(8,128)(2,1)}, bf16[4096,512]{1,0:T(8,128)(2,1)S(1)}, u32[]{:S(2)}) copy-start(bf16[4096,512]{1,0:T(8,128)(2,1)S(1)} %get-tuple-element.11.lcols) | copy-start | bytes 12582916

commit v2 on v1

--- a/solution.py
+++ b/solution.py
@@ -11,7 +11,8 @@
 PANEL = 256
 BOTH = 2 * PANEL
 GROUP = 3 * BLOCK
-CHUNKS = 4
+CHUNKS = 8
+LAG = 3
 MESH_IDS = pl.DeviceIdType.MESH
 F32 = jnp.float32
 BF16 = jnp.bfloat16
@@ -212,11 +213,12 @@
         def _():
             to_top(0).wait_recv()
 
+        short_rows = min(PANEL, chunk)
         for k in range(CHUNKS):
 
             def second(i, carry):
-                row0 = pl.multiple_of(k * chunk + i * step_rows, step_rows)
-                here = pl.ds(row0, step_rows)
+                row0 = pl.multiple_of(k * chunk + i * short_rows, short_rows)
+                here = pl.ds(row0, short_rows)
                 updated = asm[here, PANEL:BOTH] - dot_t(l_v[here, 0:PANEL], top_v[...])
                 value = dot_exact(updated, inverse2[...]).astype(BF16)
                 none = jnp.zeros_like(value)
@@ -224,7 +226,7 @@
                 l_v[here, PANEL:BOTH] = jnp.where(r * rows + row0 >= BOTH, value, none)
                 return carry
 
-            lax.fori_loop(0, chunk // step_rows, second, 0)
+            lax.fori_loop(0, chunk // short_rows, second, 0)
             for j in range(1, n_col):
                 to_col(k, j).start()
             to_half(k, l_v).start()
@@ -240,8 +242,7 @@
             for j in range(1, n_row):
                 to_top(j).wait_send()
 
-    for k in range(CHUNKS):
-
+    def pass_rows(k):
         @pl.when(slab != 0)
         def _():
             to_half(k, lrows).wait_recv()
@@ -254,6 +255,7 @@
             def _():
                 send_cols(k, lrows, None)
 
+    def pass_cols(k):
         @pl.when(z != slab)
         def _():
             here = slot_part(lcols, k)
@@ -269,6 +271,12 @@
 
             for d in range(1, fanout):
                 to_lane(k, d, here).start()
+
+    for step in range(CHUNKS + LAG):
+        if step < CHUNKS:
+            pass_rows(step)
+        if step >= LAG:
+            pass_cols(step - LAG)
 
     for k in range(CHUNKS):
         here = slot_part(lcols, k)

time: 143 us -> 129 us (0.902)
  Pallas kernels: 137 us -> 123 us
    pallas_call x1, Pallas kernels: 106 us -> 92.6 us  [body(): pl.pallas_call(functools.partial(panel_kernel, n_half, n_row, n_col), out...]
where the time goes in v2:
time: 129 us
  Pallas kernels  123 us (95%)
  local copies, waits for them, and re-layouts  5.45 us (4%)
    pallas_call x1, Pallas kernels, body(): pl.pallas_call(functools.partial(panel_kernel, n_half, n_row, n_col), out...  92.6 us
    pallas_call x1, Pallas kernels, body(): pl.pallas_call(update_kernel, out_shape=jax.ShapeDtypeStruct((rows, width...  30.5 us
    unnamed x14, local copies, waits for them, and re-layouts  5.45 us

profile of v2, /device:TPU:5, one launch (start us, length us, event | category | flops | bytes accessed | tf_op | source)
XLA Modules:
  0.0 128.6 jit_solution(6776731831009572778)
XLA Ops:
  0.0 0.1 pad_add_fusion.place
  0.1 0.0 copy-start.1
  0.1 0.9 copy-done.1
  1.0 0.0 copy-start.3
  1.0 0.9 copy-done.3
  1.9 0.0 copy-start.4
  1.9 0.9 copy-done.4
  2.8 0.0 copy-start.5
  2.8 0.7 copy-done.5
  3.5 0.0 copy-start.2
  3.5 0.0 copy-start.6
  3.5 92.6 %panels.1 = (bf16[1536,3072]{1,0:T(8,128)(2,1)}, bf16[2048,512]{1,0:T(8,128)(2,1)S(1)}, bf16[4096,512]{1,0:T(8,128)(2,1)S(1)}, bf16[2048,512]{1,0:T(8,128)(2,1)S(1)}) custom-call(bf16[2048,4096]{1,0:T(8,128)(2,1)} %bitcast.9, bf16[1536,6144]{1,0:T(8,128)(2,1)} %bitcast.7, s32[2,96,96]{2,1,0:T(8,128)S(1)} %copy-done.1, s32[2,96]{1,0:T(2,128)S(1)} %copy-done.5, ...), custom_call_target="tpu_custom_call" | custom-call | tf_op jit(solution)/shard_map/panels/pallas_call | solution.py:366
  96.1 0.0 copy-start
  96.1 2.1 %copy-done = bf16[4096,512]{1,0:T(8,128)(2,1)} copy-done((bf16[4096,512]{1,0:T(8,128)(2,1)}, bf16[4096,512]{1,0:T(8,128)(2,1)S(1)}, u32[]{:S(2)}) %copy-start) | copy-done | bytes 4194328
  98.2 0.0 copy-done.2
  98.2 0.0 copy-done.6
  98.2 30.5 %update.1 = bf16[2048,4096]{1,0:T(8,128)(2,1)} custom-call(s32[4]{0:T(128)S(1)} %pad_add_fusion.place, s32[2,96]{1,0:T(2,128)S(1)} %copy-done.6, s32[2,96,96]{2,1,0:T(8,128)S(1)} %copy-done.2, bf16[2048,4096]{1,0:T(8,128)(2,1)} %bitcast.10, bf16[1536,6144]{1,0:T(8,128)(2,1)} %bitcast.8, bf16[1536,3072]{1,0:T(8,128)(2,1)} %get-tuple-element.9.other, ...), custom_call_target="tpu_custom_call" | custom-call | tf_op jit(solution)/shard_map/update/pallas_call | solution.py:402
Async XLA Ops:
  0.1 0.9 copy-start.1
  1.0 0.9 copy-start.3
  1.9 0.9 copy-start.4
  2.8 0.7 copy-start.5
  3.5 94.7 %copy-start.2 = (s32[2,96,96]{2,1,0:T(8,128)S(1)}, s32[2,96,96]{2,1,0:T(8,128)}, u32[]{:S(2)}) copy-start(s32[2,96,96]{2,1,0:T(8,128)} %fill.3) | copy-start | bytes 221188
  3.5 94.7 %copy-start.6 = (s32[2,96]{1,0:T(2,128)S(1)}, s32[2,96]{1,0:T(2,128)}, u32[]{:S(2)}) copy-start(s32[2,96]{1,0:T(2,128)} %cmap.3) | copy-start | bytes 2308
  96.1 2.1 %copy-start = (bf16[4096,512]{1,0:T(8,128)(2,1)}, bf16[4096,512]{1,0:T(8,128)(2,1)S(1)}, u32[]{:S(2)}) copy-start(bf16[4096,512]{1,0:T(8,128)(2,1)S(1)} %get-tuple-element.11.lcols) | copy-start | bytes 12582916

commit v3 on v2

--- a/solution.py
+++ b/solution.py
@@ -11,8 +11,8 @@
 PANEL = 256
 BOTH = 2 * PANEL
 GROUP = 3 * BLOCK
-CHUNKS = 8
-LAG = 3
+CHUNKS = 16
+LAG = 5
 MESH_IDS = pl.DeviceIdType.MESH
 F32 = jnp.float32
 BF16 = jnp.bfloat16
@@ -213,12 +213,12 @@
         def _():
             to_top(0).wait_recv()
 
-        short_rows = min(PANEL, chunk)
+        span = max(PANEL, chunk)
         for k in range(CHUNKS):
 
             def second(i, carry):
-                row0 = pl.multiple_of(k * chunk + i * short_rows, short_rows)
-                here = pl.ds(row0, short_rows)
+                row0 = pl.multiple_of(k * chunk + i * step_rows, step_rows)
+                here = pl.ds(row0, step_rows)
                 updated = asm[here, PANEL:BOTH] - dot_t(l_v[here, 0:PANEL], top_v[...])
                 value = dot_exact(updated, inverse2[...]).astype(BF16)
                 none = jnp.zeros_like(value)
@@ -226,7 +226,8 @@
                 l_v[here, PANEL:BOTH] = jnp.where(r * rows + row0 >= BOTH, value, none)
                 return carry
 
-            lax.fori_loop(0, chunk // short_rows, second, 0)
+            if k * chunk % span == 0:
+                lax.fori_loop(0, span // step_rows, second, 0)
             for j in range(1, n_col):
                 to_col(k, j).start()
             to_half(k, l_v).start()

time: 129 us -> 123 us (0.953)
  Pallas kernels: 123 us -> 117 us
    pallas_call x1, Pallas kernels: 92.6 us -> 86.8 us  [body(): pl.pallas_call(functools.partial(panel_kernel, n_half, n_row, n_col), out...]
where the time goes in v3:
time: 123 us
  Pallas kernels  117 us (95%)
  local copies, waits for them, and re-layouts  5.45 us (4%)
    pallas_call x1, Pallas kernels, body(): pl.pallas_call(functools.partial(panel_kernel, n_half, n_row, n_col), out...  86.8 us
    pallas_call x1, Pallas kernels, body(): pl.pallas_call(update_kernel, out_shape=jax.ShapeDtypeStruct((rows, width...  30.4 us
    unnamed x14, local copies, waits for them, and re-layouts  5.45 us

profile of v3, /device:TPU:5, one launch (start us, length us, event | category | flops | bytes accessed | tf_op | source)
XLA Modules:
  0.0 122.7 jit_solution(8254907768092345219)
XLA Ops:
  0.0 0.1 pad_add_fusion.place
  0.1 0.0 copy-start.1
  0.1 0.9 copy-done.1
  1.0 0.0 copy-start.3
  1.0 0.9 copy-done.3
  1.9 0.0 copy-start.4
  1.9 0.9 copy-done.4
  2.8 0.0 copy-start.5
  2.8 0.7 copy-done.5
  3.5 0.0 copy-start.2
  3.5 0.0 copy-start.6
  3.5 86.8 %panels.1 = (bf16[1536,3072]{1,0:T(8,128)(2,1)}, bf16[2048,512]{1,0:T(8,128)(2,1)S(1)}, bf16[4096,512]{1,0:T(8,128)(2,1)S(1)}, bf16[2048,512]{1,0:T(8,128)(2,1)S(1)}) custom-call(bf16[2048,4096]{1,0:T(8,128)(2,1)} %bitcast.9, bf16[1536,6144]{1,0:T(8,128)(2,1)} %bitcast.7, s32[2,96,96]{2,1,0:T(8,128)S(1)} %copy-done.1, s32[2,96]{1,0:T(2,128)S(1)} %copy-done.5, ...), custom_call_target="tpu_custom_call" | custom-call | tf_op jit(solution)/shard_map/panels/pallas_call | solution.py:367
  90.2 0.0 copy-start
  90.2 2.1 %copy-done = bf16[4096,512]{1,0:T(8,128)(2,1)} copy-done((bf16[4096,512]{1,0:T(8,128)(2,1)}, bf16[4096,512]{1,0:T(8,128)(2,1)S(1)}, u32[]{:S(2)}) %copy-start) | copy-done | bytes 4194328
  92.3 0.0 copy-done.2
  92.3 0.0 copy-done.6
  92.3 30.4 %update.1 = bf16[2048,4096]{1,0:T(8,128)(2,1)} custom-call(s32[4]{0:T(128)S(1)} %pad_add_fusion.place, s32[2,96]{1,0:T(2,128)S(1)} %copy-done.6, s32[2,96,96]{2,1,0:T(8,128)S(1)} %copy-done.2, bf16[2048,4096]{1,0:T(8,128)(2,1)} %bitcast.10, bf16[1536,6144]{1,0:T(8,128)(2,1)} %bitcast.8, bf16[1536,3072]{1,0:T(8,128)(2,1)} %get-tuple-element.9.other, ...), custom_call_target="tpu_custom_call" | custom-call | tf_op jit(solution)/shard_map/update/pallas_call | solution.py:403
Async XLA Ops:
  0.1 0.9 copy-start.1
  1.0 0.9 copy-start.3
  1.9 0.9 copy-start.4
  2.8 0.7 copy-start.5
  3.5 88.8 %copy-start.2 = (s32[2,96,96]{2,1,0:T(8,128)S(1)}, s32[2,96,96]{2,1,0:T(8,128)}, u32[]{:S(2)}) copy-start(s32[2,96,96]{2,1,0:T(8,128)} %fill.3) | copy-start | bytes 221188
  3.5 88.8 %copy-start.6 = (s32[2,96]{1,0:T(2,128)S(1)}, s32[2,96]{1,0:T(2,128)}, u32[]{:S(2)}) copy-start(s32[2,96]{1,0:T(2,128)} %cmap.3) | copy-start | bytes 2308
  90.2 2.1 %copy-start = (bf16[4096,512]{1,0:T(8,128)(2,1)}, bf16[4096,512]{1,0:T(8,128)(2,1)S(1)}, u32[]{:S(2)}) copy-start(bf16[4096,512]{1,0:T(8,128)(2,1)S(1)} %get-tuple-element.11.lcols) | copy-start | bytes 12582916
